TPU v7x, 512 devices: a whole 4x8x8 slice. The times are simulated.
512 devices in a mesh: depth: 4 (over x), row: 16 (over y, core), col: 8 (over z).
Axes of the slice: x: 4, y: 8, z: 8, core: 2. Of those that a mesh axis runs over, the one named last changes fastest.
Arguments:
- latents: bfloat16 [4, 16, 8, 3, 8, 8, 8, 256], P('depth', 'row', 'col'), may hold values from -6 to 6
- neighbours: int32 [4, 16, 8, 3, 6], P('depth', 'row', 'col'), may hold values from -1 to 1535, as said below
- owners: int32 [4, 16, 8, 3, 8], P('depth', 'row', 'col'), may hold values from -1 to 255, as said below
- conv_weight: bfloat16 [27, 256, 256], P(None, None, 'row'), may hold values from -0.078125 to 0.078125
- step_embed: float32 [256], replicated, may hold values from -6 to 6
- up_weight: bfloat16 [8, 256, 128], replicated, may hold values from -0.375 to 0.375
Outputs:
- upsampled: bfloat16 [4, 16, 8, 16, 8, 8, 8, 128], P('depth', 'row', 'col')
Inputs may be any that keep to these rules, and one draw needn't show every extreme that they name: `neighbours`: entry d names the brick beside a brick's face in direction d (order -z, +z, -y, +y, -x, +x) as ((depth * 16 + row) * 8 + col) * 3 + slot; that brick lies on the same device or on the device beside it across that face. -1 where no brick is there and in every entry of an empty slot. The occupied slots of a device come first. `owners`: for an occupied slot, entry k is j * 16 + u: child k goes to slot u of the device at row j with the same depth and col; -1 in empty slots. Each device holds 1 to 3 occupied slots, and in every line of devices along row some device holds 3. Every device receives exactly 16 children, each slot once, and no device sends more than 2 children to one device.
All inputs are finite; a program needn't handle non-finite values.
Results may differ from a plain program's by a relative error of at most 0.0051.
Values may be sent and summed in bfloat16 or wider, within the bound.
No kernel may reach another device: no remote copies, remote signals or barrier semaphores. Data moves between devices by JAX's collectives and lax.ppermute only.
A program may use at most 64 MiB of HBM per device.

v0:
```python
import jax
import jax.numpy as jnp
from jax import lax
from jax.sharding import PartitionSpec as P

OCAP = 16


def with_halo(cells, sides, width):
    for axis, dim in sides:
        count = lax.axis_size(axis)
        ends = count - 1
        head = lax.slice_in_dim(cells, 0, width, axis=dim)
        tail = lax.slice_in_dim(cells, cells.shape[dim] - width, cells.shape[dim], axis=dim)
        cells = jnp.concatenate(
            [
                lax.ppermute(tail, axis, [(i, (i + 1) % count) for i in range(ends)]),
                cells,
                lax.ppermute(head, axis, [((i + 1) % count, i) for i in range(ends)]),
            ],
            axis=dim,
        )
    return cells


def normed_silu(values):
    mean_square = jnp.mean(values * values, axis=-1, keepdims=True)
    return jax.nn.silu(values * lax.rsqrt(mean_square + 1e-06))


def borrowed(local_face, remote_face, near_index, own_index, offset, slots_dev):
    owner_dev = near_index // slots_dev
    in_slot = near_index % slots_dev
    chosen = jnp.where(
        near_index < 0,
        -1,
        jnp.where(
            owner_dev == own_index,
            in_slot,
            jnp.where(owner_dev == own_index + offset, slots_dev + in_slot, -1),
        ),
    )
    picker = (chosen[:, None] == jnp.arange(2 * slots_dev, dtype=jnp.int32)[None, :]).astype(
        jnp.bfloat16
    )
    stacked = jnp.concatenate([local_face, remote_face], axis=0).reshape(2 * slots_dev, -1)
    picked = jnp.dot(picker, stacked, preferred_element_type=jnp.float32)
    return picked.astype(jnp.bfloat16).reshape(local_face.shape)


def padded_field(source, near_ids, own_index, row_count, col_count):
    slots_dev = source.shape[0]
    edge_len = source.shape[1]
    depth_faces = with_halo(jnp.stack([source[:, 0], source[:, -1]]), (("depth", 0),), 1)
    row_faces = with_halo(jnp.stack([source[:, :, 0], source[:, :, -1]]), (("row", 0),), 1)
    col_faces = with_halo(jnp.stack([source[:, :, :, 0], source[:, :, :, -1]]), (("col", 0),), 1)
    plane_size = row_count * col_count
    below_z = borrowed(
        depth_faces[2], depth_faces[0], near_ids[:, 0], own_index, -plane_size, slots_dev
    )
    above_z = borrowed(
        depth_faces[1], depth_faces[3], near_ids[:, 1], own_index, plane_size, slots_dev
    )
    below_y = borrowed(row_faces[2], row_faces[0], near_ids[:, 2], own_index, -col_count, slots_dev)
    above_y = borrowed(row_faces[1], row_faces[3], near_ids[:, 3], own_index, col_count, slots_dev)
    below_x = borrowed(col_faces[2], col_faces[0], near_ids[:, 4], own_index, -1, slots_dev)
    above_x = borrowed(col_faces[1], col_faces[3], near_ids[:, 5], own_index, 1, slots_dev)
    padded = jnp.zeros(
        (slots_dev, edge_len + 2, edge_len + 2, edge_len + 2, source.shape[-1]), jnp.bfloat16
    )
    padded = padded.at[:, 1:-1, 1:-1, 1:-1].set(source)
    padded = padded.at[:, 0, 1:-1, 1:-1].set(below_z)
    padded = padded.at[:, edge_len + 1, 1:-1, 1:-1].set(above_z)
    padded = padded.at[:, 1:-1, 0, 1:-1].set(below_y)
    padded = padded.at[:, 1:-1, edge_len + 1, 1:-1].set(above_y)
    padded = padded.at[:, 1:-1, 1:-1, 0].set(below_x)
    padded = padded.at[:, 1:-1, 1:-1, edge_len + 1].set(above_x)
    return padded


def convolve(source, weight, near_ids, own_index, row_count, col_count):
    channels = source.shape[-1]
    padded = padded_field(source, near_ids, own_index, row_count, col_count)
    weight_piece = lax.all_gather(weight, "row", axis=2, tiled=True)
    kernel = weight_piece.reshape(3, 3, 3, channels, weight_piece.shape[2])
    return lax.conv_general_dilated(
        padded,
        kernel,
        (1, 1, 1),
        "VALID",
        dimension_numbers=("NDHWC", "DHWIO", "NDHWC"),
        preferred_element_type=jnp.float32,
    )


def body(latents, neighbours, owners, conv_weight, step_embed, up_weight):
    row_count = lax.axis_size("row")
    col_count = lax.axis_size("col")
    own_row = lax.axis_index("row")
    own_index = (lax.axis_index("depth") * row_count + own_row) * col_count + lax.axis_index("col")
    latent = latents.reshape(latents.shape[3:]).astype(jnp.float32)
    slots_dev, edge_len, channels = (latent.shape[0], latent.shape[1], latent.shape[-1])
    half_len = edge_len // 2
    out_channels = up_weight.shape[-1]
    near_ids = neighbours.reshape(slots_dev, 6)
    owner_ids = owners.reshape(slots_dev * 8)
    first_input = normed_silu(latent).astype(jnp.bfloat16)
    conv_sum = (
        convolve(first_input, conv_weight, near_ids, own_index, row_count, col_count) + step_embed
    )
    refined = (latent + conv_sum).astype(jnp.bfloat16)
    expand = up_weight.transpose(1, 0, 2).reshape(channels, 8 * out_channels)
    projected = jnp.dot(
        refined.reshape(slots_dev * edge_len**3, channels),
        expand,
        preferred_element_type=jnp.float32,
    )
    projected = projected.reshape(
        slots_dev, 2, half_len, 2, half_len, 2, half_len, 2, 2, 2, out_channels
    )
    projected = projected.transpose(0, 1, 3, 5, 2, 7, 4, 8, 6, 9, 10)
    payload = projected.reshape(slots_dev * 8, edge_len**3, out_channels).astype(jnp.bfloat16)
    item_shape = payload.shape[1:]
    send_cap = (8 * slots_dev + row_count - 1) // row_count
    is_valid = owner_ids >= 0
    target_row = jnp.where(is_valid, owner_ids // OCAP, 0)
    target_slot = jnp.where(is_valid, owner_ids % OCAP, -1)
    serial = jnp.arange(slots_dev * 8, dtype=jnp.int32)
    earlier = (
        (target_row[None, :] == target_row[:, None])
        & (serial[None, :] < serial[:, None])
        & is_valid[None, :]
    )
    ranked = jnp.sum(earlier.astype(jnp.int32), axis=1)
    position = jnp.where(is_valid, target_row * send_cap + ranked, row_count * send_cap)
    outgoing = (
        jnp.zeros((row_count * send_cap,) + item_shape, jnp.bfloat16)
        .at[position]
        .set(payload, mode="drop")
    )
    labels = (
        jnp.full((row_count * send_cap,), -1, jnp.int32).at[position].set(target_slot, mode="drop")
    )
    arrived, arrived_labels = (
        lax.all_to_all(
            outgoing.reshape((row_count, send_cap) + item_shape),
            "row",
            split_axis=0,
            concat_axis=0,
            tiled=True,
        ),
        lax.all_to_all(
            labels.reshape(row_count, send_cap), "row", split_axis=0, concat_axis=0, tiled=True
        ),
    )
    arrived = arrived.reshape((row_count * send_cap,) + item_shape)
    arrived_labels = arrived_labels.reshape(row_count * send_cap)
    placed = jnp.where(arrived_labels >= 0, arrived_labels, OCAP)
    upsampled = (
        jnp.zeros((OCAP, edge_len**3, out_channels), jnp.bfloat16)
        .at[placed]
        .set(arrived, mode="drop")
    )
    return upsampled.reshape(1, 1, 1, OCAP, edge_len, edge_len, edge_len, out_channels)


def solution(mesh):
    return jax.shard_map(
        body,
        mesh=mesh,
        in_specs=(
            P("depth", "row", "col", None, None, None, None, None),
            P("depth", "row", "col", None, None),
            P("depth", "row", "col", None, None),
            P(None, None, "row"),
            P(),
            P(),
        ),
        out_specs=P("depth", "row", "col", None, None, None, None, None),
        check_vma=False,
    )
```

profile of v0, /device:TPU:198, one launch (start us, length us, event | category | flops | bytes accessed | tf_op | source)
XLA Modules:
  0.0 205.4 jit_solution(4541175386371983872)
XLA Ops:
  6.5 0.7 all-gather.2.cloned.1.call-update
  7.3 1.9 fusion.5
  9.3 1.6 fusion.4
  10.9 0.9 fusion.56
  11.8 1.3 collective-permute-start
  13.1 5.2 %collective-permute-start.1 = (bf16[1,3,8,8,256]{4,1,3,2,0:T(4,128)(2,1)}, bf16[1,3,8,8,256]{4,1,3,2,0:T(4,128)(2,1)}, u32[]{:S(2)}, u32[]{:S(2)}) collective-permute-start(bf16[1,3,8,8,256]{4,1,3,2,0:T(4,128)(2,1)} %get-tuple-element.105), channel_id=1, source_target_pairs={{128,0},{256,128},{384,256},{129,1},{257,129},{385,257},{130,2},{2... | collective-permute-start | bytes 294920 | tf_op jit(solution)/shard_map/ppermute | solution.py:19
  18.3 0.2 fusion.55
  18.5 2.1 %collective-permute-start.2 = (bf16[1,3,8,8,256]{4,1,3,2,0:T(4,128)(2,1)S(1)}, bf16[1,3,8,8,256]{4,1,3,2,0:T(4,128)(2,1)}, u32[]{:S(2)}, u32[]{:S(2)}) collective-permute-start(bf16[1,3,8,8,256]{4,1,3,2,0:T(4,128)(2,1)S(1)} %get-tuple-element.100), channel_id=1, source_target_pairs={{0,8},{8,16},{16,24},{24,32},{32,40},{40,48},{48,56},{56,64},{64,7... | collective-permute-start | bytes 294920 | tf_op jit(solution)/shard_map/ppermute | solution.py:17
  20.6 1.3 collective-permute-start.3
  21.9 0.2 fusion.54
  22.1 5.5 %collective-permute-start.4 = (bf16[1,3,8,8,256]{4,1,3,2,0:T(4,128)(2,1)S(1)}, bf16[1,3,8,8,256]{4,1,3,2,0:T(4,128)(2,1)}, u32[]{:S(2)}, u32[]{:S(2)}) collective-permute-start(bf16[1,3,8,8,256]{4,1,3,2,0:T(4,128)(2,1)S(1)} %get-tuple-element.96), channel_id=1, source_target_pairs={{0,1},{1,2},{2,3},{3,4},{4,5},{5,6},{6,7},{8,9},{9,10},{10,11},{11... | collective-permute-start | bytes 294920 | tf_op jit(solution)/shard_map/ppermute | solution.py:17
  27.7 0.1 reshape.584
  27.7 0.1 reshape.583
  27.8 0.5 fusion.40
  28.3 0.2 convert_reduce_fusion
  28.6 0.8 scatter_custom_fusion
  29.3 0.7 all_to_all.9
  30.0 10.8 %all-to-all-start = ((s32[16,1,2]{2,1,0:T(1,128)}), s32[16,1,2]{2,1,0:T(1,128)S(1)}, u32[]{:S(2)}, u32[]{:S(2)}) async-start(s32[16,1,2]{2,1,0:T(1,128)} %bitcast.88), calls=%async_computation | async-start | bytes 16384 | tf_op jit(solution)/shard_map/all_to_all | solution.py:152
  40.8 2.0 scatter.45
  42.8 0.2 copy.48
  43.0 0.3 select_reduce_fusion
  43.3 2.1 %collective-permute-start.5 = (bf16[1,3,8,8,256]{4,1,3,2,0:T(4,128)(2,1)S(1)}, bf16[1,3,8,8,256]{4,1,3,2,0:T(4,128)(2,1)S(1)}, u32[]{:S(2)}, u32[]{:S(2)}) collective-permute-start(bf16[1,3,8,8,256]{4,1,3,2,0:T(4,128)(2,1)S(1)} %get-tuple-element.97), channel_id=1, source_target_pairs={{1,0},{2,1},{3,2},{4,3},{5,4},{6,5},{7,6},{9,8},{10,9},{11,10},{12... | collective-permute-start | bytes 294920 | tf_op jit(solution)/shard_map/ppermute | solution.py:19
  45.4 1.3 convolution_convert_fusion.5
  46.7 0.7 constant_dynamic-update-slice_fusion.5
  47.4 1.2 convolution_convert_fusion.4
  48.6 0.7 constant_dynamic-update-slice_fusion.4
  49.3 1.2 convolution_convert_fusion.3
  50.5 0.7 constant_dynamic-update-slice_fusion.3
  51.2 1.2 convolution_convert_fusion.2
  52.4 0.7 constant_dynamic-update-slice_fusion.2
  53.1 1.2 convolution_convert_fusion.1
  54.3 0.7 constant_dynamic-update-slice_fusion.1
  55.0 0.3 convolution_convert_fusion
  55.3 0.7 constant_dynamic-update-slice_fusion
  56.0 0.2 all-gather.2.cloned.1.call-done
  56.3 17.9 %fusion.6 = bf16[3,8,8,8,256]{4,0,3,2,1:T(4,128)(2,1)S(1)} fusion(bf16[3,10,10,10,256]{4,0,3,2,1:T(4,128)(2,1)} %constant_dynamic-update-slice_fusion, bf16[3,3,3,256,256]{3,4,2,1,0:T(8,128)(2,1)} %bitcast.89, f32[256]{0:T(256)S(1)} %copy-done.7, bf16[1,1,1,3,8,8,8,256]{7,6,5,4,3,2,1,0:T(8,128)(2,1)S(1)} %copy-done.1), kind=kOutput, calls=%fused_computation.19 | convolution fusion | flops 5437390848 | bytes 6648832 | tf_op jit(solution)/shard_map/conv_general_dilated | solution.py:86
  74.2 1.2 convert_bitcast_fusion
  75.4 3.4 %copy.50 = bf16[3,2,2,2,4,2,4,2,4,2,128]{10,9,8,7,6,5,4,3,2,1,0:T(2,128)(2,1)S(1)} copy(bf16[3,2,2,2,4,2,4,2,4,2,128]{10,8,9,7,5,3,6,2,4,1,0:T(4,128)(2,1)S(1)} %convert_bitcast_fusion) | data formatting | bytes 6291456 | tf_op jit(solution)/shard_map/convert_element_type | solution.py:122
  78.8 2.9 %broadcast_in_dim.62 = bf16[32,512,128]{2,1,0:T(8,128)(2,1)} broadcast(bf16[]{:T(256)} %constant.330.clone.1), dimensions={} | broadcast | bytes 4194306 | tf_op jit(solution)/shard_map/broadcast_in_dim | solution.py:137
  81.7 7.6 %scatter_fusion = bf16[32,512,128]{2,1,0:T(8,128)(2,1)} fusion(bf16[32,512,128]{2,1,0:T(8,128)(2,1)} %broadcast_in_dim.62, s32[24]{0:T(128)S(1)} %copy-done.6, bf16[24,512,128]{2,1,0:T(8,128)(2,1)S(1)} %bitcast.73), kind=kCustom, calls=%fused_computation.1 | custom fusion | bytes 9437280 | tf_op jit(solution)/shard_map/scatter | solution.py:139
  89.3 7.0 %all-to-all-start.1 = ((bf16[16,2,512,128]{3,2,1,0:T(8,128)(2,1)}), bf16[16,2,512,128]{3,2,1,0:T(8,128)(2,1)}, u32[]{:S(2)}, u32[]{:S(2)}) async-start(bf16[16,2,512,128]{3,2,1,0:T(8,128)(2,1)} %bitcast.72), calls=%async_computation.1 | async-start | bytes 8388608 | tf_op jit(solution)/shard_map/all_to_all | solution.py:145
  96.3 0.5 broadcast.496
  96.8 0.7 reduce.31
  97.5 0.1 reshape.585
  97.6 93.0 %all-to-all-done.1 = bf16[16,2,512,128]{3,2,1,0:T(8,128)(2,1)} async-done(((bf16[16,2,512,128]{3,2,1,0:T(8,128)(2,1)}), bf16[16,2,512,128]{3,2,1,0:T(8,128)(2,1)}, u32[]{:S(2)}, u32[]{:S(2)}) %all-to-all-start.1) | async-done | bytes 4194336 | tf_op jit(solution)/shard_map/all_to_all | solution.py:145
  190.6 0.4 broadcast_in_dim.31
  191.0 6.3 %scatter_fusion.1 = bf16[16,512,128]{2,1,0:T(8,128)(2,1)S(1)} fusion(bf16[16,512,128]{2,1,0:T(8,128)(2,1)S(1)} %broadcast_in_dim.31, s32[32]{0:T(128)S(1)} %fusion.44, bf16[32,512,128]{2,1,0:T(8,128)(2,1)} %bitcast.42), kind=kCustom, calls=%fused_computation.2 | custom fusion | bytes 12583040 | tf_op jit(solution)/shard_map/scatter | solution.py:162
  197.3 1.3 copy-done
  (29 shorter events, 0.2 us)
Async XLA Ops:
  6.5 2.7 %copy-start.1 = (bf16[1,1,1,3,8,8,8,256]{7,6,5,4,3,2,1,0:T(8,128)(2,1)S(1)}, bf16[1,1,1,3,8,8,8,256]{7,6,5,4,3,2,1,0:T(8,128)(2,1)}, u32[]{:S(2)}) copy-start(bf16[1,1,1,3,8,8,8,256]{7,6,5,4,3,2,1,0:T(8,128)(2,1)} %param.20) | copy-start | bytes 2359300
  6.5 49.7 %all-gather.2.cloned.1.call-start = ((), (), s32[]{:S(2)}) async-start(), calls=%async_computation.2 | async-start | bytes 3760128 | tf_op jit(solution)/shard_map/all_gather | solution.py:84
  9.2 18.4 %copy-start.4 = (s32[1,1,1,3,8]{4,2,3,1,0:T(1,128)S(1)}, s32[1,1,1,3,8]{4,2,3,1,0:T(1,128)}, u32[]{:S(2)}) copy-start(s32[1,1,1,3,8]{4,2,3,1,0:T(1,128)} %param.22) | copy-start | bytes 292
  9.2 31.6 %copy-start.3 = (s32[1,1,1,3,6]{4,2,3,1,0:T(1,128)S(1)}, s32[1,1,1,3,6]{4,2,3,1,0:T(1,128)}, u32[]{:S(2)}) copy-start(s32[1,1,1,3,6]{4,2,3,1,0:T(1,128)} %param.21) | copy-start | bytes 220
  11.8 31.5 %collective-permute-start = (bf16[1,3,8,8,256]{4,1,3,2,0:T(4,128)(2,1)}, bf16[1,3,8,8,256]{4,1,3,2,0:T(4,128)(2,1)}, u32[]{:S(2)}, u32[]{:S(2)}) collective-permute-start(bf16[1,3,8,8,256]{4,1,3,2,0:T(4,128)(2,1)} %get-tuple-element.104), channel_id=1, source_target_pairs={{0,128},{128,256},{256,384},{1,129},{129,257},{257,385},{2,130},{1... | collective-permute-start | bytes 294920 | tf_op jit(solution)/shard_map/ppermute | solution.py:17
  13.1 34.4 %collective-permute-start.1 = (bf16[1,3,8,8,256]{4,1,3,2,0:T(4,128)(2,1)}, bf16[1,3,8,8,256]{4,1,3,2,0:T(4,128)(2,1)}, u32[]{:S(2)}, u32[]{:S(2)}) collective-permute-start(bf16[1,3,8,8,256]{4,1,3,2,0:T(4,128)(2,1)} %get-tuple-element.105), channel_id=1, source_target_pairs={{128,0},{256,128},{384,256},{129,1},{257,129},{385,257},{130,2},{2... | collective-permute-start | bytes 294920 | tf_op jit(solution)/shard_map/ppermute | solution.py:19
  18.5 24.3 %copy-start.2 = (bf16[8,256,128]{2,1,0:T(8,128)(2,1)S(1)}, bf16[8,256,128]{2,1,0:T(8,128)(2,1)}, u32[]{:S(2)}) copy-start(bf16[8,256,128]{2,1,0:T(8,128)(2,1)} %param.25) | copy-start | bytes 1572868
  18.5 30.8 %collective-permute-start.2 = (bf16[1,3,8,8,256]{4,1,3,2,0:T(4,128)(2,1)S(1)}, bf16[1,3,8,8,256]{4,1,3,2,0:T(4,128)(2,1)}, u32[]{:S(2)}, u32[]{:S(2)}) collective-permute-start(bf16[1,3,8,8,256]{4,1,3,2,0:T(4,128)(2,1)S(1)} %get-tuple-element.100), channel_id=1, source_target_pairs={{0,8},{8,16},{16,24},{24,32},{32,40},{40,48},{48,56},{56,64},{64,7... | collective-permute-start | bytes 294920 | tf_op jit(solution)/shard_map/ppermute | solution.py:17
  20.6 30.6 %collective-permute-start.3 = (bf16[1,3,8,8,256]{4,1,3,2,0:T(4,128)(2,1)S(1)}, bf16[1,3,8,8,256]{4,1,3,2,0:T(4,128)(2,1)}, u32[]{:S(2)}, u32[]{:S(2)}) collective-permute-start(bf16[1,3,8,8,256]{4,1,3,2,0:T(4,128)(2,1)S(1)} %get-tuple-element.101), channel_id=1, source_target_pairs={{8,0},{16,8},{24,16},{32,24},{40,32},{48,40},{56,48},{64,56},{72,6... | collective-permute-start | bytes 294920 | tf_op jit(solution)/shard_map/ppermute | solution.py:19
  22.1 31.0 %collective-permute-start.4 = (bf16[1,3,8,8,256]{4,1,3,2,0:T(4,128)(2,1)S(1)}, bf16[1,3,8,8,256]{4,1,3,2,0:T(4,128)(2,1)}, u32[]{:S(2)}, u32[]{:S(2)}) collective-permute-start(bf16[1,3,8,8,256]{4,1,3,2,0:T(4,128)(2,1)S(1)} %get-tuple-element.96), channel_id=1, source_target_pairs={{0,1},{1,2},{2,3},{3,4},{4,5},{5,6},{6,7},{8,9},{9,10},{10,11},{11... | collective-permute-start | bytes 294920 | tf_op jit(solution)/shard_map/ppermute | solution.py:17
  28.5 12.3 %copy-start.5 = (s32[24]{0:T(128)}, s32[24]{0:T(128)S(1)}, u32[]{:S(2)}) copy-start(s32[24]{0:T(128)S(1)} %fusion.43) | copy-start | bytes 292
  30.0 59.2 %all-to-all-start = ((s32[16,1,2]{2,1,0:T(1,128)}), s32[16,1,2]{2,1,0:T(1,128)S(1)}, u32[]{:S(2)}, u32[]{:S(2)}) async-start(s32[16,1,2]{2,1,0:T(1,128)} %bitcast.88), calls=%async_computation | async-start | bytes 16384 | tf_op jit(solution)/shard_map/all_to_all | solution.py:152
  43.3 11.7 %collective-permute-start.5 = (bf16[1,3,8,8,256]{4,1,3,2,0:T(4,128)(2,1)S(1)}, bf16[1,3,8,8,256]{4,1,3,2,0:T(4,128)(2,1)S(1)}, u32[]{:S(2)}, u32[]{:S(2)}) collective-permute-start(bf16[1,3,8,8,256]{4,1,3,2,0:T(4,128)(2,1)S(1)} %get-tuple-element.97), channel_id=1, source_target_pairs={{1,0},{2,1},{3,2},{4,3},{5,4},{6,5},{7,6},{9,8},{10,9},{11,10},{12... | collective-permute-start | bytes 294920 | tf_op jit(solution)/shard_map/ppermute | solution.py:19
  45.4 10.8 %copy-start.7 = (f32[256]{0:T(256)S(1)}, f32[256]{0:T(256)}, u32[]{:S(2)}) copy-start(f32[256]{0:T(256)} %param.24) | copy-start | bytes 3076
  78.8 2.9 %copy-start.6 = (s32[24]{0:T(128)S(1)}, s32[24]{0:T(128)}, u32[]{:S(2)}) copy-start(s32[24]{0:T(128)} %copy-done.5) | copy-start | bytes 292
  89.3 101.3 %all-to-all-start.1 = ((bf16[16,2,512,128]{3,2,1,0:T(8,128)(2,1)}), bf16[16,2,512,128]{3,2,1,0:T(8,128)(2,1)}, u32[]{:S(2)}, u32[]{:S(2)}) async-start(bf16[16,2,512,128]{3,2,1,0:T(8,128)(2,1)} %bitcast.72), calls=%async_computation.1 | async-start | bytes 8388608 | tf_op jit(solution)/shard_map/all_to_all | solution.py:145
  197.3 1.3 copy-start
Sparse Core Ops, SparseCore 0:
  9.5 46.7 all-gather.1
where the time goes:
time: 206 us; the launch traced here: 205 us
  waiting for transfers between devices  94 us (46%)
  starting transfers between devices  35.2 us (17%)
  local copies, waits for them, and re-layouts  31.9 us (15%)
  matrix products  25.4 us (12%)
  between operations  13.7 us (7%)
  other arithmetic  5.3 us (3%)
    all_to_all x1, waiting for transfers between devices, body(): lax.all_to_all(outgoing.reshape((row_count, send_cap) + item_shape), 'row...  93 us
    conv_general_dilated x1, matrix products, convolve(): lax.conv_general_dilated(padded, kernel, (1, 1, 1), 'VALID', dimension_nu...  17.9 us
    all_to_all x1, starting transfers between devices, body(): lax.all_to_all(labels.reshape(row_count, send_cap), 'row', split_axis=0,...  10.8 us
    ppermute x3, starting transfers between devices, with_halo(): lax.ppermute(tail, axis, [(i, (i + 1) % count) for i in range(ends)])  8.86 us
    ppermute x3, starting transfers between devices, with_halo(): lax.ppermute(head, axis, [((i + 1) % count, i) for i in range(ends)])  8.57 us
    scatter x1, local copies, waits for them, and re-layouts, body(): outgoing = jnp.zeros((row_count * send_cap,) + item_shape, jnp.bfloat16)....  7.56 us
    all_to_all x1, starting transfers between devices, body(): lax.all_to_all(outgoing.reshape((row_count, send_cap) + item_shape), 'row...  7 us
    dot_general x6, matrix products, borrowed(): picked = jnp.dot(picker, stacked, preferred_element_type=jnp.float32)  6.28 us
  transfers between devices with their start and end apart: 9, of which 2 were waited for; matrix products, arithmetic and copies ran while one was open for 26% of the time, Pallas kernels for 0%

commit v1 on v0

--- a/solution.py
+++ b/solution.py
@@ -4,6 +4,29 @@
 from jax.sharding import PartitionSpec as P
 
 OCAP = 16
+
+
+def split_up(x, dim, size):
+    shape = x.shape
+    parts = x.reshape(*shape[:dim], size, shape[dim] // size, *shape[dim + 1 :])
+    return jnp.moveaxis(parts, dim, 0)
+
+
+def laid_out(blocks, dim):
+    blocks = jnp.moveaxis(blocks, 0, dim)
+    dims = blocks.shape
+    return blocks.reshape(*dims[:dim], dims[dim] * dims[dim + 1], *dims[dim + 2 :])
+
+
+def exchange_in_pairs(x, axis, split_dim, concat_dim):
+    devices, index = (lax.axis_size(axis), lax.axis_index(axis))
+    blocks = split_up(x, split_dim, devices)
+    outs = [blocks[index]]
+    for lap in range(1, devices):
+        sent = blocks[index ^ lap]
+        outs.append(lax.ppermute(sent, axis, [(i, i ^ lap) for i in range(devices)]))
+    blocks = jnp.stack(outs)[index ^ jnp.arange(devices)]
+    return laid_out(blocks, concat_dim)
 
 
 def with_halo(cells, sides, width):
@@ -142,13 +165,7 @@
         jnp.full((row_count * send_cap,), -1, jnp.int32).at[position].set(target_slot, mode="drop")
     )
     arrived, arrived_labels = (
-        lax.all_to_all(
-            outgoing.reshape((row_count, send_cap) + item_shape),
-            "row",
-            split_axis=0,
-            concat_axis=0,
-            tiled=True,
-        ),
+        exchange_in_pairs(outgoing.reshape((row_count, send_cap) + item_shape), "row", 0, 0),
         lax.all_to_all(
             labels.reshape(row_count, send_cap), "row", split_axis=0, concat_axis=0, tiled=True
         ),

time: 206 us -> 269 us (1.31)
  the two profiles are of different devices: /device:TPU:198 before, /device:TPU:5 now
where the time goes in v1:
time: 269 us; the launch traced here: 267 us
  starting transfers between devices  122 us (45%)
  local copies, waits for them, and re-layouts  52.1 us (19%)
  waiting for transfers between devices  47.9 us (18%)
  matrix products  25.4 us (9%)
  between operations  13.9 us (5%)
  other arithmetic  6.03 us (2%)
    ppermute x15, starting transfers between devices, exchange_in_pairs(): lax.ppermute(sent, axis, [(i, i ^ lap) for i in range(devices)])  95.4 us
    ppermute x15, waiting for transfers between devices, exchange_in_pairs(): lax.ppermute(sent, axis, [(i, i ^ lap) for i in range(devices)])  44.2 us
    conv_general_dilated x1, matrix products, convolve(): lax.conv_general_dilated(padded, kernel, (1, 1, 1), 'VALID', dimension_nu...  17.9 us
    unnamed x28, local copies, waits for them, and re-layouts  12.6 us
    ppermute x3, starting transfers between devices, with_halo(): lax.ppermute(tail, axis, [(i, (i + 1) % count) for i in range(ends)])  11.8 us
    all_to_all x1, starting transfers between devices, body(): lax.all_to_all(labels.reshape(row_count, send_cap), 'row', split_axis=0,...  9.16 us
    scatter x1, local copies, waits for them, and re-layouts, body(): outgoing = jnp.zeros((row_count * send_cap,) + item_shape, jnp.bfloat16)....  6.92 us
    scatter x1, local copies, waits for them, and re-layouts, body(): upsampled = jnp.zeros((OCAP, edge_len ** 3, out_channels), jnp.bfloat16)....  6.28 us
  transfers between devices with their start and end apart: 23, of which 7 were waited for; matrix products, arithmetic and copies ran while one was open for 26% of the time, Pallas kernels for 0%

profile of v1, /device:TPU:5, one launch (start us, length us, event | category | flops | bytes accessed | tf_op | source)
XLA Modules:
  0.0 267.5 jit_solution(6846783893799844644)
XLA Ops:
  7.3 1.9 fusion.5
  9.2 2.9 %fusion.4 = bf16[3,8,8,8,256]{4,0,3,2,1:T(4,128)(2,1)S(1)} fusion(f32[3,8,8,8]{0,3,2,1:T(8,128)S(1)} %add_rsqrt_fusion, bf16[1,1,1,3,8,8,8,256]{7,6,5,4,3,2,1,0:T(8,128)(2,1)} %param.20), kind=kLoop, calls=%fused_computation.18 | loop fusion | flops 2752512 | bytes 1579008 | tf_op jit(solution)/shard_map/convert_element_type | solution.py:130
  12.1 0.9 fusion.57
  13.0 2.8 %collective-permute-start = (bf16[1,3,8,8,256]{4,1,3,2,0:T(4,128)(2,1)}, bf16[1,3,8,8,256]{4,1,3,2,0:T(4,128)(2,1)}, u32[]{:S(2)}, u32[]{:S(2)}) collective-permute-start(bf16[1,3,8,8,256]{4,1,3,2,0:T(4,128)(2,1)} %get-tuple-element.120), channel_id=1, source_target_pairs={{0,128},{128,256},{256,384},{1,129},{129,257},{257,385},{2,130},{1... | collective-permute-start | bytes 294920 | tf_op jit(solution)/shard_map/ppermute | solution.py:40
  15.8 2.5 collective-permute-start.1
  18.5 4.3 %collective-permute-start.2 = (bf16[1,3,8,8,256]{4,1,3,2,0:T(4,128)(2,1)S(1)}, bf16[1,3,8,8,256]{4,1,3,2,0:T(4,128)(2,1)}, u32[]{:S(2)}, u32[]{:S(2)}) collective-permute-start(bf16[1,3,8,8,256]{4,1,3,2,0:T(4,128)(2,1)S(1)} %get-tuple-element.116), channel_id=1, source_target_pairs={{0,8},{8,16},{16,24},{24,32},{32,40},{40,48},{48,56},{56,64},{64,7... | collective-permute-start | bytes 294920 | tf_op jit(solution)/shard_map/ppermute | solution.py:40
  22.9 1.9 collective-permute-start.3
  25.0 4.6 %collective-permute-start.4 = (bf16[1,3,8,8,256]{4,1,3,2,0:T(4,128)(2,1)S(1)}, bf16[1,3,8,8,256]{4,1,3,2,0:T(4,128)(2,1)}, u32[]{:S(2)}, u32[]{:S(2)}) collective-permute-start(bf16[1,3,8,8,256]{4,1,3,2,0:T(4,128)(2,1)S(1)} %get-tuple-element.112), channel_id=1, source_target_pairs={{0,1},{1,2},{2,3},{3,4},{4,5},{5,6},{6,7},{8,9},{9,10},{10,11},{11... | collective-permute-start | bytes 294920 | tf_op jit(solution)/shard_map/ppermute | solution.py:40
  31.4 9.2 %all-to-all-start = ((s32[16,1,2]{2,1,0:T(1,128)}), s32[16,1,2]{2,1,0:T(1,128)S(1)}, u32[]{:S(2)}, u32[]{:S(2)}) async-start(s32[16,1,2]{2,1,0:T(1,128)} %bitcast.2), calls=%async_computation | async-start | bytes 16384 | tf_op jit(solution)/shard_map/all_to_all | solution.py:169
  40.6 2.0 scatter.45
  43.2 1.5 collective-permute-start.5
  44.7 1.3 convolution_convert_fusion.5
  46.7 1.2 convolution_convert_fusion.4
  48.6 1.2 convolution_convert_fusion.3
  50.5 1.2 convolution_convert_fusion.2
  52.4 1.2 convolution_convert_fusion.1
  55.3 3.1 %all-gather.2.cloned.1.call-done = bf16[27,256,256]{1,2,0:T(8,128)(2,1)} async-done(((bf16[27,256,16]{1,2,0:T(8,128)(2,1)}), bf16[27,256,256]{1,2,0:T(8,128)(2,1)}) %all-gather.2.cloned.1.call-update) | async-done | bytes 3538960 | tf_op jit(solution)/shard_map/all_gather | solution.py:107
  58.3 17.9 %fusion.6 = bf16[3,8,8,8,256]{4,0,3,2,1:T(4,128)(2,1)S(1)} fusion(bf16[3,10,10,10,256]{4,0,3,2,1:T(4,128)(2,1)} %constant_dynamic-update-slice_fusion, bf16[3,3,3,256,256]{3,4,2,1,0:T(8,128)(2,1)} %bitcast.153, f32[256]{0:T(256)S(1)} %copy-done.5, bf16[1,1,1,3,8,8,8,256]{7,6,5,4,3,2,1,0:T(8,128)(2,1)S(1)} %copy-done.1), kind=kOutput, calls=%fused_computation.20 | convolution fusion | flops 5437390848 | bytes 6648832 | tf_op jit(solution)/shard_map/conv_general_dilated | solution.py:109
  76.2 1.2 convert_bitcast_fusion
  77.4 3.4 %copy.50 = bf16[3,2,2,2,4,2,4,2,4,2,128]{10,9,8,7,6,5,4,3,2,1,0:T(2,128)(2,1)S(1)} copy(bf16[3,2,2,2,4,2,4,2,4,2,128]{10,8,9,7,5,3,6,2,4,1,0:T(4,128)(2,1)S(1)} %convert_bitcast_fusion) | data formatting | bytes 6291456 | tf_op jit(solution)/shard_map/convert_element_type | solution.py:145
  80.9 2.9 %broadcast_in_dim.63 = bf16[32,512,128]{2,1,0:T(8,128)(2,1)} broadcast(bf16[]{:T(256)} %constant.344.clone.1), dimensions={} | broadcast | bytes 4194306 | tf_op jit(solution)/shard_map/broadcast_in_dim | solution.py:160
  83.8 6.9 %scatter_fusion = bf16[32,512,128]{2,1,0:T(8,128)(2,1)} fusion(bf16[32,512,128]{2,1,0:T(8,128)(2,1)} %broadcast_in_dim.63, s32[24]{0:T(128)S(1)} %fusion.43, bf16[24,512,128]{2,1,0:T(8,128)(2,1)S(1)} %bitcast.137), kind=kCustom, calls=%fused_computation.2 | custom fusion | bytes 9437280 | tf_op jit(solution)/shard_map/scatter | solution.py:162
  90.7 3.8 %dynamic-slice_bitcast_fusion = (bf16[1,2,512,128]{3,2,1,0:T(8,128)(2,1)S(1)}, bf16[1,2,512,128]{3,2,1,0:T(8,128)(2,1)S(1)}, bf16[1,2,512,128]{3,2,1,0:T(8,128)(...) fusion(bf16[16,1,2,512,128]{4,3,2,0,1:T(8,128)(2,1)} %bitcast.1, ...), kind=kLoop, calls=%fused_computation.55 | loop fusion | bytes 8388672 | tf_op jit(solution)/shard_map/squeeze | solution.py:26
  94.5 2.2 collective-permute-start.6
  98.0 4.2 %collective-permute-start.7 = (bf16[1,2,512,128]{3,2,1,0:T(8,128)(2,1)}, bf16[1,2,512,128]{3,2,1,0:T(8,128)(2,1)S(1)}, u32[]{:S(2)}, u32[]{:S(2)}) collective-permute-start(bf16[1,2,512,128]{3,2,1,0:T(8,128)(2,1)} %get-tuple-element.108), channel_id=1, source_target_pairs={{0,16},{8,24},{16,0},{24,8},{32,48},{40,56},{48,32},{56,40},{64,80... | collective-permute-start | bytes 786440 | tf_op jit(solution)/shard_map/ppermute | solution.py:27
  102.3 1.9 collective-permute-start.8
  104.2 3.3 %collective-permute-start.9 = (bf16[1,2,512,128]{3,2,1,0:T(8,128)(2,1)S(1)}, bf16[1,2,512,128]{3,2,1,0:T(8,128)(2,1)S(1)}, u32[]{:S(2)}, u32[]{:S(2)}) collective-permute-start(bf16[1,2,512,128]{3,2,1,0:T(8,128)(2,1)S(1)} %get-tuple-element.106), channel_id=1, source_target_pairs={{0,32},{8,40},{16,48},{24,56},{32,0},{40,8},{48,16},{56,24},{64,96... | collective-permute-start | bytes 786440 | tf_op jit(solution)/shard_map/ppermute | solution.py:27
  107.4 3.5 %collective-permute-start.10 = (bf16[1,2,512,128]{3,2,1,0:T(8,128)(2,1)S(1)}, bf16[1,2,512,128]{3,2,1,0:T(8,128)(2,1)S(1)}, u32[]{:S(2)}, u32[]{:S(2)}) collective-permute-start(bf16[1,2,512,128]{3,2,1,0:T(8,128)(2,1)S(1)} %get-tuple-element.105), channel_id=1, source_target_pairs={{0,40},{8,32},{16,56},{24,48},{32,8},{40,0},{48,24},{56,16},{64,10... | collective-permute-start | bytes 786440 | tf_op jit(solution)/shard_map/ppermute | solution.py:27
  111.0 4.0 %collective-permute-start.11 = (bf16[1,2,512,128]{3,2,1,0:T(8,128)(2,1)S(1)}, bf16[1,2,512,128]{3,2,1,0:T(8,128)(2,1)S(1)}, u32[]{:S(2)}, u32[]{:S(2)}) collective-permute-start(bf16[1,2,512,128]{3,2,1,0:T(8,128)(2,1)S(1)} %get-tuple-element.104), channel_id=1, source_target_pairs={{0,48},{8,56},{16,32},{24,40},{32,16},{40,24},{48,0},{56,8},{64,11... | collective-permute-start | bytes 786440 | tf_op jit(solution)/shard_map/ppermute | solution.py:27
  115.0 1.7 bitcast_dynamic-update-slice_fusion.14
  116.7 3.0 %collective-permute-start.12 = (bf16[1,2,512,128]{3,2,1,0:T(8,128)(2,1)S(1)}, bf16[1,2,512,128]{3,2,1,0:T(8,128)(2,1)S(1)}, u32[]{:S(2)}, u32[]{:S(2)}) collective-permute-start(bf16[1,2,512,128]{3,2,1,0:T(8,128)(2,1)S(1)} %get-tuple-element.103), channel_id=1, source_target_pairs={{0,56},{8,48},{16,40},{24,32},{32,24},{40,16},{48,8},{56,0},{64,12... | collective-permute-start | bytes 786440 | tf_op jit(solution)/shard_map/ppermute | solution.py:27
  120.9 4.8 %collective-permute-start.13 = (bf16[1,2,512,128]{3,2,1,0:T(8,128)(2,1)S(1)}, bf16[1,2,512,128]{3,2,1,0:T(8,128)(2,1)S(1)}, u32[]{:S(2)}, u32[]{:S(2)}) collective-permute-start(bf16[1,2,512,128]{3,2,1,0:T(8,128)(2,1)S(1)} %get-tuple-element.102), channel_id=1, source_target_pairs={{0,64},{8,72},{16,80},{24,88},{32,96},{40,104},{48,112},{56,120},{... | collective-permute-start | bytes 786440 | tf_op jit(solution)/shard_map/ppermute | solution.py:27
  126.5 28.4 %collective-permute-start.14 = (bf16[1,2,512,128]{3,2,1,0:T(8,128)(2,1)S(1)}, bf16[1,2,512,128]{3,2,1,0:T(8,128)(2,1)S(1)}, u32[]{:S(2)}, u32[]{:S(2)}) collective-permute-start(bf16[1,2,512,128]{3,2,1,0:T(8,128)(2,1)S(1)} %get-tuple-element.101), channel_id=1, source_target_pairs={{0,72},{8,64},{16,88},{24,80},{32,104},{40,96},{48,120},{56,112},{... | collective-permute-start | bytes 786440 | tf_op jit(solution)/shard_map/ppermute | solution.py:27
  155.6 2.3 collective-permute-start.15
  158.6 23.4 %collective-permute-start.16 = (bf16[1,2,512,128]{3,2,1,0:T(8,128)(2,1)S(1)}, bf16[1,2,512,128]{3,2,1,0:T(8,128)(2,1)S(1)}, u32[]{:S(2)}, u32[]{:S(2)}) collective-permute-start(bf16[1,2,512,128]{3,2,1,0:T(8,128)(2,1)S(1)} %get-tuple-element.99), channel_id=1, source_target_pairs={{0,88},{8,80},{16,72},{24,64},{32,120},{40,112},{48,104},{56,96},{... | collective-permute-start | bytes 786440 | tf_op jit(solution)/shard_map/ppermute | solution.py:27
  182.7 4.4 %collective-permute-start.17 = (bf16[1,2,512,128]{3,2,1,0:T(8,128)(2,1)S(1)}, bf16[1,2,512,128]{3,2,1,0:T(8,128)(2,1)S(1)}, u32[]{:S(2)}, u32[]{:S(2)}) collective-permute-start(bf16[1,2,512,128]{3,2,1,0:T(8,128)(2,1)S(1)} %get-tuple-element.98), channel_id=1, source_target_pairs={{0,96},{8,104},{16,112},{24,120},{32,64},{40,72},{48,80},{56,88},{... | collective-permute-start | bytes 786440 | tf_op jit(solution)/shard_map/ppermute | solution.py:27
  187.8 2.9 %collective-permute-start.18 = (bf16[1,2,512,128]{3,2,1,0:T(8,128)(2,1)S(1)}, bf16[1,2,512,128]{3,2,1,0:T(8,128)(2,1)S(1)}, u32[]{:S(2)}, u32[]{:S(2)}) collective-permute-start(bf16[1,2,512,128]{3,2,1,0:T(8,128)(2,1)S(1)} %get-tuple-element.97), channel_id=1, source_target_pairs={{0,104},{8,96},{16,120},{24,112},{32,72},{40,64},{48,88},{56,80},{... | collective-permute-start | bytes 786440 | tf_op jit(solution)/shard_map/ppermute | solution.py:27
  190.7 0.7 bitcast_dynamic-update-slice_fusion.7
  191.5 3.7 %collective-permute-start.19 = (bf16[1,2,512,128]{3,2,1,0:T(8,128)(2,1)S(1)}, bf16[1,2,512,128]{3,2,1,0:T(8,128)(2,1)S(1)}, u32[]{:S(2)}, u32[]{:S(2)}) collective-permute-start(bf16[1,2,512,128]{3,2,1,0:T(8,128)(2,1)S(1)} %get-tuple-element.96), channel_id=1, source_target_pairs={{0,112},{8,120},{16,96},{24,104},{32,80},{40,88},{48,64},{56,72},{... | collective-permute-start | bytes 786440 | tf_op jit(solution)/shard_map/ppermute | solution.py:27
  196.0 3.4 %collective-permute-start.20 = (bf16[1,2,512,128]{3,2,1,0:T(8,128)(2,1)S(1)}, bf16[1,2,512,128]{3,2,1,0:T(8,128)(2,1)S(1)}, u32[]{:S(2)}, u32[]{:S(2)}) collective-permute-start(bf16[1,2,512,128]{3,2,1,0:T(8,128)(2,1)S(1)} %get-tuple-element.95), channel_id=1, source_target_pairs={{0,120},{8,112},{16,104},{24,96},{32,88},{40,80},{48,72},{56,64},{... | collective-permute-start | bytes 786440 | tf_op jit(solution)/shard_map/ppermute | solution.py:27
  200.1 21.0 %collective-permute-done.16 = bf16[1,2,512,128]{3,2,1,0:T(8,128)(2,1)S(1)} collective-permute-done((bf16[1,2,512,128]{3,2,1,0:T(8,128)(2,1)S(1)}, bf16[1,2,512,128]{3,2,1,0:T(8,128)(2,1)S(1)}, u32[]{:S(2)}, u32[]{:S(2)}) %collective-permute-start.16) | collective-permute-done | bytes 262176 | tf_op jit(solution)/shard_map/ppermute | solution.py:27
  221.8 4.9 %collective-permute-done.17 = bf16[1,2,512,128]{3,2,1,0:T(8,128)(2,1)S(1)} collective-permute-done((bf16[1,2,512,128]{3,2,1,0:T(8,128)(2,1)S(1)}, bf16[1,2,512,128]{3,2,1,0:T(8,128)(2,1)S(1)}, u32[]{:S(2)}, u32[]{:S(2)}) %collective-permute-start.17) | collective-permute-done | bytes 262176 | tf_op jit(solution)/shard_map/ppermute | solution.py:27
  227.4 4.9 %collective-permute-done.18 = bf16[1,2,512,128]{3,2,1,0:T(8,128)(2,1)S(1)} collective-permute-done((bf16[1,2,512,128]{3,2,1,0:T(8,128)(2,1)S(1)}, bf16[1,2,512,128]{3,2,1,0:T(8,128)(2,1)S(1)}, u32[]{:S(2)}, u32[]{:S(2)}) %collective-permute-start.18) | collective-permute-done | bytes 262176 | tf_op jit(solution)/shard_map/ppermute | solution.py:27
  233.0 8.0 %collective-permute-done.19 = bf16[1,2,512,128]{3,2,1,0:T(8,128)(2,1)S(1)} collective-permute-done((bf16[1,2,512,128]{3,2,1,0:T(8,128)(2,1)S(1)}, bf16[1,2,512,128]{3,2,1,0:T(8,128)(2,1)S(1)}, u32[]{:S(2)}, u32[]{:S(2)}) %collective-permute-start.19) | collective-permute-done | bytes 262176 | tf_op jit(solution)/shard_map/ppermute | solution.py:27
  241.8 4.9 %collective-permute-done.20 = bf16[1,2,512,128]{3,2,1,0:T(8,128)(2,1)S(1)} collective-permute-done((bf16[1,2,512,128]{3,2,1,0:T(8,128)(2,1)S(1)}, bf16[1,2,512,128]{3,2,1,0:T(8,128)(2,1)S(1)}, u32[]{:S(2)}, u32[]{:S(2)}) %collective-permute-start.20) | collective-permute-done | bytes 262176 | tf_op jit(solution)/shard_map/ppermute | solution.py:27
  247.4 5.2 %gather_fusion = bf16[16,2,512,128]{3,2,1,0:T(8,128)(2,1)} fusion(bf16[16,2,512,128]{3,2,1,0:T(8,128)(2,1)} %bitcast.138, s32[1024]{0:T(1024)S(1)} %pad_clamp_fusion), kind=kCustom, calls=%fused_computation | custom fusion | bytes 8388672 | tf_op jit(solution)/shard_map/gather | solution.py:28
  253.0 6.3 %scatter_fusion.1 = bf16[16,512,128]{2,1,0:T(8,128)(2,1)S(1)} fusion(bf16[16,512,128]{2,1,0:T(8,128)(2,1)S(1)} %broadcast_in_dim.31, s32[32]{0:T(128)S(1)} %fusion.44, bf16[32,512,128]{2,1,0:T(8,128)(2,1)} %bitcast.136), kind=kCustom, calls=%fused_computation.3 | custom fusion | bytes 12583040 | tf_op jit(solution)/shard_map/scatter | solution.py:179
  259.3 1.3 copy-done
  (72 shorter events, 19.6 us)
Async XLA Ops:
  6.5 23.2 %copy-start.4 = (s32[1,1,1,3,8]{4,2,3,1,0:T(1,128)S(1)}, s32[1,1,1,3,8]{4,2,3,1,0:T(1,128)}, u32[]{:S(2)}) copy-start(s32[1,1,1,3,8]{4,2,3,1,0:T(1,128)} %param.22) | copy-start | bytes 292
  6.5 34.1 %copy-start.3 = (s32[1,1,1,3,6]{4,2,3,1,0:T(1,128)S(1)}, s32[1,1,1,3,6]{4,2,3,1,0:T(1,128)}, u32[]{:S(2)}) copy-start(s32[1,1,1,3,6]{4,2,3,1,0:T(1,128)} %param.21) | copy-start | bytes 220
  6.5 51.8 %all-gather.2.cloned.1.call-start = ((), (), s32[]{:S(2)}) async-start(), calls=%async_computation.1 | async-start | bytes 3760128 | tf_op jit(solution)/shard_map/all_gather | solution.py:107
  9.2 33.4 %copy-start.2 = (bf16[8,256,128]{2,1,0:T(8,128)(2,1)S(1)}, bf16[8,256,128]{2,1,0:T(8,128)(2,1)}, u32[]{:S(2)}) copy-start(bf16[8,256,128]{2,1,0:T(8,128)(2,1)} %param.25) | copy-start | bytes 1572868
  13.0 30.2 %collective-permute-start = (bf16[1,3,8,8,256]{4,1,3,2,0:T(4,128)(2,1)}, bf16[1,3,8,8,256]{4,1,3,2,0:T(4,128)(2,1)}, u32[]{:S(2)}, u32[]{:S(2)}) collective-permute-start(bf16[1,3,8,8,256]{4,1,3,2,0:T(4,128)(2,1)} %get-tuple-element.120), channel_id=1, source_target_pairs={{0,128},{128,256},{256,384},{1,129},{129,257},{257,385},{2,130},{1... | collective-permute-start | bytes 294920 | tf_op jit(solution)/shard_map/ppermute | solution.py:40
  15.8 30.9 %collective-permute-start.1 = (bf16[1,3,8,8,256]{4,1,3,2,0:T(4,128)(2,1)}, bf16[1,3,8,8,256]{4,1,3,2,0:T(4,128)(2,1)}, u32[]{:S(2)}, u32[]{:S(2)}) collective-permute-start(bf16[1,3,8,8,256]{4,1,3,2,0:T(4,128)(2,1)} %get-tuple-element.121), channel_id=1, source_target_pairs={{128,0},{256,128},{384,256},{129,1},{257,129},{385,257},{130,2},{2... | collective-permute-start | bytes 294920 | tf_op jit(solution)/shard_map/ppermute | solution.py:42
  18.5 30.0 %collective-permute-start.2 = (bf16[1,3,8,8,256]{4,1,3,2,0:T(4,128)(2,1)S(1)}, bf16[1,3,8,8,256]{4,1,3,2,0:T(4,128)(2,1)}, u32[]{:S(2)}, u32[]{:S(2)}) collective-permute-start(bf16[1,3,8,8,256]{4,1,3,2,0:T(4,128)(2,1)S(1)} %get-tuple-element.116), channel_id=1, source_target_pairs={{0,8},{8,16},{16,24},{24,32},{32,40},{40,48},{48,56},{56,64},{64,7... | collective-permute-start | bytes 294920 | tf_op jit(solution)/shard_map/ppermute | solution.py:40
  22.9 27.6 %collective-permute-start.3 = (bf16[1,3,8,8,256]{4,1,3,2,0:T(4,128)(2,1)S(1)}, bf16[1,3,8,8,256]{4,1,3,2,0:T(4,128)(2,1)}, u32[]{:S(2)}, u32[]{:S(2)}) collective-permute-start(bf16[1,3,8,8,256]{4,1,3,2,0:T(4,128)(2,1)S(1)} %get-tuple-element.117), channel_id=1, source_target_pairs={{8,0},{16,8},{24,16},{32,24},{40,32},{48,40},{56,48},{64,56},{72,6... | collective-permute-start | bytes 294920 | tf_op jit(solution)/shard_map/ppermute | solution.py:42
  25.0 27.3 %collective-permute-start.4 = (bf16[1,3,8,8,256]{4,1,3,2,0:T(4,128)(2,1)S(1)}, bf16[1,3,8,8,256]{4,1,3,2,0:T(4,128)(2,1)}, u32[]{:S(2)}, u32[]{:S(2)}) collective-permute-start(bf16[1,3,8,8,256]{4,1,3,2,0:T(4,128)(2,1)S(1)} %get-tuple-element.112), channel_id=1, source_target_pairs={{0,1},{1,2},{2,3},{3,4},{4,5},{5,6},{6,7},{8,9},{9,10},{10,11},{11... | collective-permute-start | bytes 294920 | tf_op jit(solution)/shard_map/ppermute | solution.py:40
  31.4 65.3 %all-to-all-start = ((s32[16,1,2]{2,1,0:T(1,128)}), s32[16,1,2]{2,1,0:T(1,128)S(1)}, u32[]{:S(2)}, u32[]{:S(2)}) async-start(s32[16,1,2]{2,1,0:T(1,128)} %bitcast.2), calls=%async_computation | async-start | bytes 16384 | tf_op jit(solution)/shard_map/all_to_all | solution.py:169
  40.6 17.7 %copy-start.1 = (bf16[1,1,1,3,8,8,8,256]{7,6,5,4,3,2,1,0:T(8,128)(2,1)S(1)}, bf16[1,1,1,3,8,8,8,256]{7,6,5,4,3,2,1,0:T(8,128)(2,1)}, u32[]{:S(2)}) copy-start(bf16[1,1,1,3,8,8,8,256]{7,6,5,4,3,2,1,0:T(8,128)(2,1)} %param.20) | copy-start | bytes 2359300
  42.6 15.7 %copy-start.5 = (f32[256]{0:T(256)S(1)}, f32[256]{0:T(256)}, u32[]{:S(2)}) copy-start(f32[256]{0:T(256)} %param.24) | copy-start | bytes 3076
  43.2 11.1 %collective-permute-start.5 = (bf16[1,3,8,8,256]{4,1,3,2,0:T(4,128)(2,1)S(1)}, bf16[1,3,8,8,256]{4,1,3,2,0:T(4,128)(2,1)S(1)}, u32[]{:S(2)}, u32[]{:S(2)}) collective-permute-start(bf16[1,3,8,8,256]{4,1,3,2,0:T(4,128)(2,1)S(1)} %get-tuple-element.113), channel_id=1, source_target_pairs={{1,0},{2,1},{3,2},{4,3},{5,4},{6,5},{7,6},{9,8},{10,9},{11,10},{12... | collective-permute-start | bytes 294920 | tf_op jit(solution)/shard_map/ppermute | solution.py:42
  94.5 16.4 %collective-permute-start.6 = (bf16[1,2,512,128]{3,2,1,0:T(8,128)(2,1)}, bf16[1,2,512,128]{3,2,1,0:T(8,128)(2,1)}, u32[]{:S(2)}, u32[]{:S(2)}) collective-permute-start(bf16[1,2,512,128]{3,2,1,0:T(8,128)(2,1)} %get-tuple-element.109), channel_id=1, source_target_pairs={{0,8},{8,0},{16,24},{24,16},{32,40},{40,32},{48,56},{56,48},{64,72... | collective-permute-start | bytes 786440 | tf_op jit(solution)/shard_map/ppermute | solution.py:27
  98.0 18.7 %collective-permute-start.7 = (bf16[1,2,512,128]{3,2,1,0:T(8,128)(2,1)}, bf16[1,2,512,128]{3,2,1,0:T(8,128)(2,1)S(1)}, u32[]{:S(2)}, u32[]{:S(2)}) collective-permute-start(bf16[1,2,512,128]{3,2,1,0:T(8,128)(2,1)} %get-tuple-element.108), channel_id=1, source_target_pairs={{0,16},{8,24},{16,0},{24,8},{32,48},{40,56},{48,32},{56,40},{64,80... | collective-permute-start | bytes 786440 | tf_op jit(solution)/shard_map/ppermute | solution.py:27
  102.3 18.6 %collective-permute-start.8 = (bf16[1,2,512,128]{3,2,1,0:T(8,128)(2,1)S(1)}, bf16[1,2,512,128]{3,2,1,0:T(8,128)(2,1)S(1)}, u32[]{:S(2)}, u32[]{:S(2)}) collective-permute-start(bf16[1,2,512,128]{3,2,1,0:T(8,128)(2,1)S(1)} %get-tuple-element.107), channel_id=1, source_target_pairs={{0,24},{8,16},{16,8},{24,0},{32,56},{40,48},{48,40},{56,32},{64,88... | collective-permute-start | bytes 786440 | tf_op jit(solution)/shard_map/ppermute | solution.py:27
  104.2 22.3 %collective-permute-start.9 = (bf16[1,2,512,128]{3,2,1,0:T(8,128)(2,1)S(1)}, bf16[1,2,512,128]{3,2,1,0:T(8,128)(2,1)S(1)}, u32[]{:S(2)}, u32[]{:S(2)}) collective-permute-start(bf16[1,2,512,128]{3,2,1,0:T(8,128)(2,1)S(1)} %get-tuple-element.106), channel_id=1, source_target_pairs={{0,32},{8,40},{16,48},{24,56},{32,0},{40,8},{48,16},{56,24},{64,96... | collective-permute-start | bytes 786440 | tf_op jit(solution)/shard_map/ppermute | solution.py:27
  107.4 48.1 %collective-permute-start.10 = (bf16[1,2,512,128]{3,2,1,0:T(8,128)(2,1)S(1)}, bf16[1,2,512,128]{3,2,1,0:T(8,128)(2,1)S(1)}, u32[]{:S(2)}, u32[]{:S(2)}) collective-permute-start(bf16[1,2,512,128]{3,2,1,0:T(8,128)(2,1)S(1)} %get-tuple-element.105), channel_id=1, source_target_pairs={{0,40},{8,32},{16,56},{24,48},{32,8},{40,0},{48,24},{56,16},{64,10... | collective-permute-start | bytes 786440 | tf_op jit(solution)/shard_map/ppermute | solution.py:27
  111.0 47.6 %collective-permute-start.11 = (bf16[1,2,512,128]{3,2,1,0:T(8,128)(2,1)S(1)}, bf16[1,2,512,128]{3,2,1,0:T(8,128)(2,1)S(1)}, u32[]{:S(2)}, u32[]{:S(2)}) collective-permute-start(bf16[1,2,512,128]{3,2,1,0:T(8,128)(2,1)S(1)} %get-tuple-element.104), channel_id=1, source_target_pairs={{0,48},{8,56},{16,32},{24,40},{32,16},{40,24},{48,0},{56,8},{64,11... | collective-permute-start | bytes 786440 | tf_op jit(solution)/shard_map/ppermute | solution.py:27
  116.7 66.1 %collective-permute-start.12 = (bf16[1,2,512,128]{3,2,1,0:T(8,128)(2,1)S(1)}, bf16[1,2,512,128]{3,2,1,0:T(8,128)(2,1)S(1)}, u32[]{:S(2)}, u32[]{:S(2)}) collective-permute-start(bf16[1,2,512,128]{3,2,1,0:T(8,128)(2,1)S(1)} %get-tuple-element.103), channel_id=1, source_target_pairs={{0,56},{8,48},{16,40},{24,32},{32,24},{40,16},{48,8},{56,0},{64,12... | collective-permute-start | bytes 786440 | tf_op jit(solution)/shard_map/ppermute | solution.py:27
  120.9 66.9 %collective-permute-start.13 = (bf16[1,2,512,128]{3,2,1,0:T(8,128)(2,1)S(1)}, bf16[1,2,512,128]{3,2,1,0:T(8,128)(2,1)S(1)}, u32[]{:S(2)}, u32[]{:S(2)}) collective-permute-start(bf16[1,2,512,128]{3,2,1,0:T(8,128)(2,1)S(1)} %get-tuple-element.102), channel_id=1, source_target_pairs={{0,64},{8,72},{16,80},{24,88},{32,96},{40,104},{48,112},{56,120},{... | collective-permute-start | bytes 786440 | tf_op jit(solution)/shard_map/ppermute | solution.py:27
  126.5 65.0 %collective-permute-start.14 = (bf16[1,2,512,128]{3,2,1,0:T(8,128)(2,1)S(1)}, bf16[1,2,512,128]{3,2,1,0:T(8,128)(2,1)S(1)}, u32[]{:S(2)}, u32[]{:S(2)}) collective-permute-start(bf16[1,2,512,128]{3,2,1,0:T(8,128)(2,1)S(1)} %get-tuple-element.101), channel_id=1, source_target_pairs={{0,72},{8,64},{16,88},{24,80},{32,104},{40,96},{48,120},{56,112},{... | collective-permute-start | bytes 786440 | tf_op jit(solution)/shard_map/ppermute | solution.py:27
  155.6 40.4 %collective-permute-start.15 = (bf16[1,2,512,128]{3,2,1,0:T(8,128)(2,1)S(1)}, bf16[1,2,512,128]{3,2,1,0:T(8,128)(2,1)S(1)}, u32[]{:S(2)}, u32[]{:S(2)}) collective-permute-start(bf16[1,2,512,128]{3,2,1,0:T(8,128)(2,1)S(1)} %get-tuple-element.100), channel_id=1, source_target_pairs={{0,80},{8,88},{16,64},{24,72},{32,112},{40,120},{48,96},{56,104},{... | collective-permute-start | bytes 786440 | tf_op jit(solution)/shard_map/ppermute | solution.py:27
  158.6 62.5 %collective-permute-start.16 = (bf16[1,2,512,128]{3,2,1,0:T(8,128)(2,1)S(1)}, bf16[1,2,512,128]{3,2,1,0:T(8,128)(2,1)S(1)}, u32[]{:S(2)}, u32[]{:S(2)}) collective-permute-start(bf16[1,2,512,128]{3,2,1,0:T(8,128)(2,1)S(1)} %get-tuple-element.99), channel_id=1, source_target_pairs={{0,88},{8,80},{16,72},{24,64},{32,120},{40,112},{48,104},{56,96},{... | collective-permute-start | bytes 786440 | tf_op jit(solution)/shard_map/ppermute | solution.py:27
  182.7 43.9 %collective-permute-start.17 = (bf16[1,2,512,128]{3,2,1,0:T(8,128)(2,1)S(1)}, bf16[1,2,512,128]{3,2,1,0:T(8,128)(2,1)S(1)}, u32[]{:S(2)}, u32[]{:S(2)}) collective-permute-start(bf16[1,2,512,128]{3,2,1,0:T(8,128)(2,1)S(1)} %get-tuple-element.98), channel_id=1, source_target_pairs={{0,96},{8,104},{16,112},{24,120},{32,64},{40,72},{48,80},{56,88},{... | collective-permute-start | bytes 786440 | tf_op jit(solution)/shard_map/ppermute | solution.py:27
  187.8 44.5 %collective-permute-start.18 = (bf16[1,2,512,128]{3,2,1,0:T(8,128)(2,1)S(1)}, bf16[1,2,512,128]{3,2,1,0:T(8,128)(2,1)S(1)}, u32[]{:S(2)}, u32[]{:S(2)}) collective-permute-start(bf16[1,2,512,128]{3,2,1,0:T(8,128)(2,1)S(1)} %get-tuple-element.97), channel_id=1, source_target_pairs={{0,104},{8,96},{16,120},{24,112},{32,72},{40,64},{48,88},{56,80},{... | collective-permute-start | bytes 786440 | tf_op jit(solution)/shard_map/ppermute | solution.py:27
  191.5 49.6 %collective-permute-start.19 = (bf16[1,2,512,128]{3,2,1,0:T(8,128)(2,1)S(1)}, bf16[1,2,512,128]{3,2,1,0:T(8,128)(2,1)S(1)}, u32[]{:S(2)}, u32[]{:S(2)}) collective-permute-start(bf16[1,2,512,128]{3,2,1,0:T(8,128)(2,1)S(1)} %get-tuple-element.96), channel_id=1, source_target_pairs={{0,112},{8,120},{16,96},{24,104},{32,80},{40,88},{48,64},{56,72},{... | collective-permute-start | bytes 786440 | tf_op jit(solution)/shard_map/ppermute | solution.py:27
  196.0 50.7 %collective-permute-start.20 = (bf16[1,2,512,128]{3,2,1,0:T(8,128)(2,1)S(1)}, bf16[1,2,512,128]{3,2,1,0:T(8,128)(2,1)S(1)}, u32[]{:S(2)}, u32[]{:S(2)}) collective-permute-start(bf16[1,2,512,128]{3,2,1,0:T(8,128)(2,1)S(1)} %get-tuple-element.95), channel_id=1, source_target_pairs={{0,120},{8,112},{16,104},{24,96},{32,88},{40,80},{48,72},{56,64},{... | collective-permute-start | bytes 786440 | tf_op jit(solution)/shard_map/ppermute | solution.py:27
  259.3 1.3 copy-start
Sparse Core Ops, SparseCore 0:
  9.5 48.7 all-gather.1
